TPU v7x, 32 devices: a whole 2x2x4 slice. The times are simulated.
32 devices in a mesh: span: 8 (over z, x), cross: 4 (over y, core).
Axes of the slice: x: 2, y: 2, z: 4, core: 2. Of those that a mesh axis runs over, the one named last changes fastest.
Arguments:
- velocity: float32 [3, 512, 16, 128], P(None, 'span', 'cross'), may hold values from -6 to 6
- viscosity: float32 [512, 16, 128], P('span', 'cross'), may hold values from 0.02 to 0.4
Outputs:
- advanced: float32 [3, 512, 16, 128], P(None, 'span', 'cross')
All inputs are finite; a program needn't handle non-finite values.
Results may differ from a plain program's by a relative error of at most 0.0001.
Values sent between devices are 32-bit elements; how exact they have to be, the bound alone decides.
A program may use at most 64 MiB of HBM per device.

v0:
```python
import jax
import jax.numpy as jnp
import numpy as np
from jax import lax
from jax.experimental import pallas as pl
from jax.experimental.pallas import tpu as pltpu
from jax.sharding import PartitionSpec as P

MESH = pl.DeviceIdType.MESH
TIME_STEP = 0.1
FAR = 5
RANK = 8


def symbols(length):
    w = 2.0 * np.pi * np.arange(length) / length
    k1 = (14 / 9 * np.sin(w) + 1 / 18 * np.sin(2 * w)) / (1 + 2 / 3 * np.cos(w))
    k2 = (24 / 11 * (1 - np.cos(w)) + 3 / 22 * (1 - np.cos(2 * w))) / (1 + 4 / 11 * np.cos(w))
    return k1, k2


def triple(table):
    high = table.astype(jnp.bfloat16)
    low = (table - high.astype(np.float64)).astype(jnp.bfloat16)
    return np.concatenate([high, low, high], axis=1).astype(np.float32)


def parts(values):
    high = values.astype(jnp.bfloat16)
    low = (values - high.astype(jnp.float32)).astype(jnp.bfloat16)
    return jnp.concatenate([high, high, low], axis=0)


def block_form(table, cells, rank):
    length = table[0].shape[0]
    kernels = [np.fft.ifft(symbol).real for symbol in table]
    offset = np.arange(cells)[:, None] - np.arange(cells)[None, :]
    own = np.concatenate([h[offset % length] for h in kernels])
    left = np.concatenate([h[(offset + cells) % length] for h in kernels])
    right = np.concatenate([h[(offset - cells) % length] for h in kernels])
    to_right = np.linalg.svd(left)[2][:rank]
    to_left = np.linalg.svd(right)[2][:rank]
    sums = np.concatenate([to_right, to_left])
    apply = np.concatenate([own, left @ to_right.T, right @ to_left.T], axis=1)
    return triple(sums), triple(apply)


def turn(values, shift):
    axis = values.ndim - 1
    return pltpu.roll(values, shift % values.shape[axis], axis)


def wide(values):
    return jnp.concatenate([values[i] for i in range(values.shape[0])], axis=-1)


def tall(values, count):
    n = values.shape[-1] // count
    return jnp.stack([values[:, i * n:(i + 1) * n] for i in range(count)])


def stream_pair(values):
    up_one, down_one = turn(values, -1), turn(values, 1)
    up_two, down_two = turn(values, -2), turn(values, 2)
    first = (8.0 * (up_one - down_one) - (up_two - down_two)) * (1.0 / 12.0)
    curve = (16.0 * (up_one + down_one) - (up_two + down_two) - 30.0 * values) * (1.0 / 12.0)
    return first, curve


def stream_first(values):
    return (8.0 * (turn(values, -1) - turn(values, 1)) - (turn(values, -2) - turn(values, 2))) * (1.0 / 12.0)


def cross_slope(p):
    n = p.shape[0]
    return (8.0 * (p[3:n - 1] - p[1:n - 3]) - (p[4:] - p[:n - 4])) * (1.0 / 12.0)


def cross_curve(p):
    n = p.shape[0]
    return (16.0 * (p[3:n - 1] + p[1:n - 3]) - (p[4:] + p[:n - 4]) - 30.0 * p[2:n - 2]) * (1.0 / 12.0)


def beside(p):
    mid = p[1:p.shape[0] - 1]
    return turn(mid, 1) + turn(mid, -1) + p[2:] + p[:p.shape[0] - 2]


def kernel(spans, crosses, vel_hbm, visc_hbm, table_hbm, out, vel, visc, table, load_sem,
           vx, za, zao, sx, zb, zbo, cx, zc, zco, nu_ref, send_sem, recv_sem):
    a, c = lax.axis_index("span"), lax.axis_index("cross")
    rows, cells = nu_ref.shape[0], nu_ref.shape[1]
    ra = rc = RANK
    loads = [
        pltpu.make_async_copy(source, target, load_sem.at[i])
        for i, (source, target) in enumerate([(vel_hbm, vel), (visc_hbm, visc), (table_hbm, table)])
    ]
    for load in loads:
        load.start()
    n_sums = 2 * RANK
    sums_a = table.at[0:n_sums]
    sums_c = table.at[n_sums:2 * n_sums]
    form_a = table.at[2 * n_sums:2 * n_sums + 2 * cells]
    form_c = table.at[2 * n_sums + 2 * cells:]

    def device(da, dc):
        return lax.rem(a + (da + spans), spans), lax.rem(c + (dc + crosses), crosses)

    def there(dc, action):
        if dc == 0:
            action()
        else:
            pl.when((c + dc >= 0) & (c + dc < crosses))(action)

    def clear(dc, refs):
        def action():
            for ref in refs:
                ref[...] = jnp.zeros(ref.shape, ref.dtype)

        pl.when((c + dc < 0) | (c + dc >= crosses))(action)

    barrier = pltpu.get_barrier_semaphore()
    greeted = [(da, dc) for da in (-1, 0, 1) for dc in (-2, -1, 0, 1, 2) if (da, dc) != (0, 0)]
    for da, dc in greeted:
        pl.semaphore_signal(barrier, inc=1, device_id=device(da, dc), device_id_type=MESH)

    def send(number, section, src, dst, da, dc):
        copy = pltpu.make_async_remote_copy(
            src_ref=src, dst_ref=dst, send_sem=send_sem.at[section, number],
            recv_sem=recv_sem.at[section, number], device_id=device(da, dc), device_id_type=MESH,
        )
        there(dc, copy.start)
        return copy, dc

    def arrive(copies):
        for copy, dc in copies:
            there(-dc, copy.wait_recv)

    def inside(values, first):
        kept_rows = []
        for i in range(values.shape[0]):
            number = first + i
            if number < 0:
                kept_rows.append(jnp.where(c * rows + number >= 0, values[i], 0.0))
            elif number >= rows:
                kept_rows.append(jnp.where(c * rows + number < rows * crosses, values[i], 0.0))
            else:
                kept_rows.append(values[i])
        return jnp.stack(kept_rows)

    def dot(left, right):
        rest = jnp.zeros((left.shape[1] - right.shape[0], right.shape[1]), right.dtype)
        right = jnp.concatenate([right, rest], axis=0)
        return jnp.dot(left.astype(jnp.bfloat16), right, preferred_element_type=jnp.float32)

    low, high = FAR, FAR + rows
    total = rows + 2 * FAR
    clear(-1, [vx.at[:, :, 0:2], sx.at[:, 0:2], cx.at[:, low - rows:low], zc.at[:, :, low - rows:low]])
    clear(1, [vx.at[:, :, rows + 2:], sx.at[:, rows + 2:], cx.at[:, high:high + rows], zc.at[:, :, high:high + rows]])
    clear(-2, [cx.at[:, 0:1], zc.at[:, :, 0:1]])
    clear(2, [cx.at[:, total - 1:], zc.at[:, :, total - 1:]])
    for load in loads:
        load.wait()
    for y in range(rows):
        own = pl.ds(y, cells, stride=rows)
        for k in range(3):
            vx[0, k, y + 2] = vel[k, own, :]
        nu_ref[y] = visc[own, :]

    def start(t, first, last, number):
        ends = slice(first * rows, last * rows)
        sent = [
            send(number, t, vx.at[t, first:last, rows:rows + 2], vx.at[t, first:last, 0:2], 0, 1),
            send(number + 1, t, vx.at[t, first:last, 2:4], vx.at[t, first:last, rows + 2:rows + 4], 0, -1),
        ]
        values = vx[t, first:last, 2:rows + 2]
        values = values.reshape((last - first) * rows, cells, values.shape[-1])
        edge = dot(sums_a[...], parts(wide(values)))
        zao[t, 0, ends] = tall(edge[:ra], values.shape[0])
        zao[t, 1, ends] = tall(edge[ra:], values.shape[0])
        sent += [
            send(number + 2, t, zao.at[t, 0, ends], za.at[t, 0, ends], 1, 0),
            send(number + 3, t, zao.at[t, 1, ends], za.at[t, 1, ends], -1, 0),
        ]
        return sent

    def deliver(k, result):
        for y in range(rows):
            out[k, pl.ds(y, cells, stride=rows), :] = result[y]

    kept = []
    for t in range(2):
        if not t:
            pl.semaphore_wait(barrier, len(greeted))
            started = start(0, 0, 3, 0)
        copies = started
        base = vx[t, :, 2:rows + 2]
        flat = wide(base.reshape(3 * rows, cells, base.shape[-1]))
        slope_x, curve_x = stream_pair(base.reshape(3 * rows, cells, base.shape[-1]))
        nu = nu_ref[...]
        early = [
            nu * curve_x[k * rows:(k + 1) * rows] - base[0] * slope_x[k * rows:(k + 1) * rows]
            for k in range(3)
        ]
        arrive(copies)
        kept += copies
        met = jnp.concatenate([flat, wide(za[t, 0]), wide(za[t, 1])], axis=0)
        pair = dot(form_a[...], parts(met))
        slope_z = tall(pair[:cells], 3 * rows)
        curve_z = tall(pair[cells:], 3 * rows)
        section = [None] * 3
        copies = []
        for k in (2, 1, 0):
            padded = vx[t, k]
            at = slice(k * rows, (k + 1) * rows)
            rate = early[k] + nu * (cross_curve(padded) + curve_z[at]) - (
                base[1] * cross_slope(padded) + base[2] * slope_z[at])
            if t:
                section[k] = 0.5 * vx[0, k, 2:rows + 2] + 0.5 * (base[k] + TIME_STEP * rate)
            else:
                section[k] = base[k] + TIME_STEP * rate
            if k == 2:
                flat = wide(section[2])
                edge = dot(sums_a[...], parts(flat))
                zbo[t, 0] = tall(edge[:ra], rows)
                zbo[t, 1] = tall(edge[ra:], rows)
                copies += [
                    send(6, t, zbo.at[t, 0], zb.at[t, 0], 1, 0),
                    send(7, t, zbo.at[t, 1], zb.at[t, 1], -1, 0),
                ]
            if k == 1:
                sx[t, 2:rows + 2] = section[1]
                copies += [
                    send(4, t, sx.at[t, rows:rows + 2], sx.at[t, 0:2], 0, 1),
                    send(5, t, sx.at[t, 2:4], sx.at[t, rows + 2:rows + 4], 0, -1),
                ]
        joined = stream_first(section[0])
        arrive(copies)
        kept += copies
        met = jnp.concatenate([flat, wide(zb[t, 0]), wide(zb[t, 1])], axis=0)
        source = joined + cross_slope(sx[t]) + tall(dot(form_a[:cells], parts(met)), rows)
        cx[t, low:high] = source
        copies = [
            send(8, t, cx.at[t, low:high], cx.at[t, low - rows:low], 0, 1),
            send(9, t, cx.at[t, low:high], cx.at[t, high:high + rows], 0, -1),
            send(10, t, cx.at[t, high - 1:high], cx.at[t, 0:1], 0, 2),
            send(11, t, cx.at[t, low:low + 1], cx.at[t, high + rows:high + rows + 1], 0, -2),
        ]
        edge = dot(sums_c[...], parts(wide(source)))
        number = 12
        for side in range(2):
            zco[t, side] = tall(edge[side * rc:(side + 1) * rc], rows)
            da = 1 - 2 * side
            copies += [
                send(number, t, zco.at[t, side], zc.at[t, side, low:high], da, 0),
                send(number + 1, t, zco.at[t, side], zc.at[t, side, low - rows:low], da, 1),
                send(number + 2, t, zco.at[t, side], zc.at[t, side, high:high + rows], da, -1),
                send(number + 3, t, zco.at[t, side, rows - 1:rows], zc.at[t, side, 0:1], da, 2),
                send(number + 4, t, zco.at[t, side, 0:1], zc.at[t, side, high + rows:high + rows + 1], da, -2),
            ]
            number += 5
        arrive(copies)
        kept += copies
        joint = jnp.concatenate([cx[t], zc[t, 0], zc[t, 1]], axis=1)
        columns = joint.shape[-1]
        joint = parts(wide(joint))
        powers = dot(form_c[:4 * cells], joint)
        t0, t1, t2, t3 = [tall(powers[i * cells:(i + 1) * cells], total) for i in range(4)]
        x = inside(t2[1:total - 1] + beside(t3), 1 - FAR)
        x = inside(t1[2:total - 2] + beside(x), 2 - FAR)
        scalar = inside(t0[3:total - 3] + beside(x), 3 - FAR)
        results = [section[0] + stream_first(scalar[2:rows + 2]), section[1] + cross_slope(scalar)]
        for k in range(2):
            if t:
                deliver(k, results[k])
            else:
                vx[1, k, 2:rows + 2] = results[k]
        if not t:
            started = start(1, 0, 2, 0)
        slopes = dot(form_c[4 * cells:], joint[:, 2 * columns:(total - 2) * columns])
        d0, d1, d2, d3 = [tall(slopes[i * cells:(i + 1) * cells], total - 4) for i in range(4)]
        n = total - 4
        x = inside(d2[1:n - 1] + beside(d3), 3 - FAR)
        x = inside(d1[2:n - 2] + beside(x), 4 - FAR)
        slope = d0[3:n - 3] + beside(x)
        if t:
            deliver(2, section[2] + slope)
        else:
            vx[1, 2, 2:rows + 2] = section[2] + slope
            started = started + start(1, 2, 3, 22)
    for copy, dc in kept:
        there(dc, copy.wait_send)


def solution(mesh):
    spans, crosses = mesh.shape["span"], mesh.shape["cross"]

    def per_device(velocity, viscosity):
        _, cells, rows, columns = velocity.shape
        k1, k2 = symbols(cells * spans)
        g = 1.0 / (4.0 + k2)
        sums_a, form_a = block_form([1j * k1, -k2 + 0j], cells, 8)
        powers = [g ** (m + 1) + 0j for m in range(4)]
        sums_c, form_c = block_form(powers + [1j * k1 * p for p in powers], cells, RANK)
        table = np.concatenate([
            np.pad(part, ((0, 0), (0, form_c.shape[1] - part.shape[1])))
            for part in (sums_a, sums_c, form_a, form_c)
        ])
        table = np.pad(table, ((0, 0), (0, -table.shape[1] % 128)))
        total = rows + 2 * FAR
        f32 = jnp.float32
        hbm = pl.BlockSpec(memory_space=pltpu.HBM)
        vmem = pl.BlockSpec(memory_space=pltpu.VMEM)
        result = pl.pallas_call(
            lambda *refs: kernel(spans, crosses, *refs),
            out_shape=jax.ShapeDtypeStruct((3, cells * rows, columns), f32),
            in_specs=[hbm] * 3,
            out_specs=vmem,
            scratch_shapes=[
                pltpu.VMEM((3, cells * rows, columns), f32),
                pltpu.VMEM((cells * rows, columns), f32),
                pltpu.VMEM(table.shape, f32),
                pltpu.SemaphoreType.DMA((3,)),
                pltpu.VMEM((2, 3, rows + 4, cells, columns), f32),
                pltpu.VMEM((2, 2, 3 * rows, 8, columns), f32),
                pltpu.VMEM((2, 2, 3 * rows, 8, columns), f32),
                pltpu.VMEM((2, rows + 4, cells, columns), f32),
                pltpu.VMEM((2, 2, rows, 8, columns), f32),
                pltpu.VMEM((2, 2, rows, 8, columns), f32),
                pltpu.VMEM((2, total, cells, columns), f32),
                pltpu.VMEM((2, 2, total, RANK, columns), f32),
                pltpu.VMEM((2, 2, rows, RANK, columns), f32),
                pltpu.VMEM((rows, cells, columns), f32),
                pltpu.SemaphoreType.DMA((2, 26)),
                pltpu.SemaphoreType.DMA((2, 26)),
            ],
            compiler_params=pltpu.CompilerParams(
                collective_id=0, has_side_effects=True, vmem_limit_bytes=63 * 1024 * 1024
            ),
        )(
            velocity.reshape(3, cells * rows, columns), viscosity.reshape(cells * rows, columns),
            jnp.asarray(table),
        )
        return result.reshape(3, cells, rows, columns)

    return jax.shard_map(
        per_device,
        mesh=mesh,
        in_specs=(P(None, "span", "cross", None), P("span", "cross", None)),
        out_specs=P(None, "span", "cross", None),
        check_vma=False,
    )
```

profile of v0, /device:TPU:0, one launch (start us, length us, event | category | flops | bytes accessed | tf_op | source)
XLA Modules:
  0.0 41.9 jit_solution(9359620357974357048)
XLA Ops:
  0.0 40.1 %shard_map.37 = f32[3,256,128]{2,1,0:T(8,128)} custom-call(f32[3,256,128]{2,1,0:T(8,128)} %bitcast.4, f32[256,128]{1,0:T(8,128)} %bitcast.5, f32[672,256]{1,0:T(8,128)} %constant.2.clone.refs_2_), custom_call_target="tpu_custom_call" | custom-call | tf_op jit(solution)/shard_map/pallas_call | solution.py:314
  40.1 1.8 %copy.5 = f32[3,64,4,128]{3,2,1,0:T(4,128)} copy(f32[3,64,4,128]{3,2,1,0:T(4,128)} %bitcast.3) | data formatting | bytes 786432
where the time goes:
time: 42.1 us; the launch traced here: 41.9 us
  Pallas kernels  40.1 us (95%)
  local copies, waits for them, and re-layouts  1.77 us (4%)
    pallas_call x1, Pallas kernels, per_device(): pl.pallas_call(lambda *refs: kernel(spans, crosses, *refs), out_shape=jax...  40.1 us
    unnamed x1, local copies, waits for them, and re-layouts  1.77 us

commit v1 on v0

--- a/solution.py
+++ b/solution.py
@@ -240,12 +240,7 @@
         met = jnp.concatenate([flat, wide(zb[t, 0]), wide(zb[t, 1])], axis=0)
         source = joined + cross_slope(sx[t]) + tall(dot(form_a[:cells], parts(met)), rows)
         cx[t, low:high] = source
-        copies = [
-            send(8, t, cx.at[t, low:high], cx.at[t, low - rows:low], 0, 1),
-            send(9, t, cx.at[t, low:high], cx.at[t, high:high + rows], 0, -1),
-            send(10, t, cx.at[t, high - 1:high], cx.at[t, 0:1], 0, 2),
-            send(11, t, cx.at[t, low:low + 1], cx.at[t, high + rows:high + rows + 1], 0, -2),
-        ]
+        copies = []
         edge = dot(sums_c[...], parts(wide(source)))
         number = 12
         for side in range(2):
@@ -259,6 +254,12 @@
                 send(number + 4, t, zco.at[t, side, 0:1], zc.at[t, side, high + rows:high + rows + 1], da, -2),
             ]
             number += 5
+        copies += [
+            send(8, t, cx.at[t, low:high], cx.at[t, low - rows:low], 0, 1),
+            send(9, t, cx.at[t, low:high], cx.at[t, high:high + rows], 0, -1),
+            send(10, t, cx.at[t, high - 1:high], cx.at[t, 0:1], 0, 2),
+            send(11, t, cx.at[t, low:low + 1], cx.at[t, high + rows:high + rows + 1], 0, -2),
+        ]
         arrive(copies)
         kept += copies
         joint = jnp.concatenate([cx[t], zc[t, 0], zc[t, 1]], axis=1)

time: 42.1 us -> 42.1 us (level)
  no operation moved by 1% of the time
where the time goes in v1:
time: 42.1 us; the launch traced here: 41.9 us
  Pallas kernels  40.1 us (95%)
  local copies, waits for them, and re-layouts  1.77 us (4%)
    pallas_call x1, Pallas kernels, per_device(): pl.pallas_call(lambda *refs: kernel(spans, crosses, *refs), out_shape=jax...  40.1 us
    unnamed x1, local copies, waits for them, and re-layouts  1.77 us

profile of v1, /device:TPU:0, one launch (start us, length us, event | category | flops | bytes accessed | tf_op | source)
XLA Modules:
  0.0 41.9 jit_solution(7207534063200274294)
XLA Ops:
  0.0 40.1 %shard_map.37 = f32[3,256,128]{2,1,0:T(8,128)} custom-call(f32[3,256,128]{2,1,0:T(8,128)} %bitcast.4, f32[256,128]{1,0:T(8,128)} %bitcast.5, f32[672,256]{1,0:T(8,128)} %constant.2.clone.refs_2_), custom_call_target="tpu_custom_call" | custom-call | tf_op jit(solution)/shard_map/pallas_call | solution.py:315
  40.1 1.8 %copy.5 = f32[3,64,4,128]{3,2,1,0:T(4,128)} copy(f32[3,64,4,128]{3,2,1,0:T(4,128)} %bitcast.3) | data formatting | bytes 786432

commit v2 on v0

--- a/solution.py
+++ b/solution.py
@@ -167,17 +167,22 @@
             vx[0, k, y + 2] = vel[k, own, :]
         nu_ref[y] = visc[own, :]
 
+    def sums_of(t, first, last):
+        ends = slice(first * rows, last * rows)
+        values = vx[t, first:last, 2:rows + 2]
+        values = values.reshape((last - first) * rows, cells, values.shape[-1])
+        edge = dot(sums_a[...], parts(wide(values)))
+        zao[t, 0, ends] = tall(edge[:ra], values.shape[0])
+        zao[t, 1, ends] = tall(edge[ra:], values.shape[0])
+
     def start(t, first, last, number):
         ends = slice(first * rows, last * rows)
         sent = [
             send(number, t, vx.at[t, first:last, rows:rows + 2], vx.at[t, first:last, 0:2], 0, 1),
             send(number + 1, t, vx.at[t, first:last, 2:4], vx.at[t, first:last, rows + 2:rows + 4], 0, -1),
         ]
-        values = vx[t, first:last, 2:rows + 2]
-        values = values.reshape((last - first) * rows, cells, values.shape[-1])
-        edge = dot(sums_a[...], parts(wide(values)))
-        zao[t, 0, ends] = tall(edge[:ra], values.shape[0])
-        zao[t, 1, ends] = tall(edge[ra:], values.shape[0])
+        if t:
+            sums_of(t, first, last)
         sent += [
             send(number + 2, t, zao.at[t, 0, ends], za.at[t, 0, ends], 1, 0),
             send(number + 3, t, zao.at[t, 1, ends], za.at[t, 1, ends], -1, 0),
@@ -191,6 +196,7 @@
     kept = []
     for t in range(2):
         if not t:
+            sums_of(0, 0, 3)
             pl.semaphore_wait(barrier, len(greeted))
             started = start(0, 0, 3, 0)
         copies = started

time: 42.1 us -> 41.9 us (level)
  no operation moved by 1% of the time
where the time goes in v2:
time: 41.9 us; the launch traced here: 41.7 us
  Pallas kernels  39.9 us (95%)
  local copies, waits for them, and re-layouts  1.77 us (4%)
    pallas_call x1, Pallas kernels, per_device(): pl.pallas_call(lambda *refs: kernel(spans, crosses, *refs), out_shape=jax...  39.9 us
    unnamed x1, local copies, waits for them, and re-layouts  1.77 us

profile of v2, /device:TPU:0, one launch (start us, length us, event | category | flops | bytes accessed | tf_op | source)
XLA Modules:
  0.0 41.7 jit_solution(17561799189030494313)
XLA Ops:
  0.0 39.9 %shard_map.37 = f32[3,256,128]{2,1,0:T(8,128)} custom-call(f32[3,256,128]{2,1,0:T(8,128)} %bitcast.4, f32[256,128]{1,0:T(8,128)} %bitcast.5, f32[672,256]{1,0:T(8,128)} %constant.2.clone.refs_2_), custom_call_target="tpu_custom_call" | custom-call | tf_op jit(solution)/shard_map/pallas_call | solution.py:320
  39.9 1.8 %copy.5 = f32[3,64,4,128]{3,2,1,0:T(4,128)} copy(f32[3,64,4,128]{3,2,1,0:T(4,128)} %bitcast.3) | data formatting | bytes 786432
